TPU v7x, 32 devices: a whole 2x2x4 slice. The times are simulated.
32 devices in a mesh: dp: 4 (over y, x), expert: 8 (over z, core).
Axes of the slice: x: 2, y: 2, z: 4, core: 2. Of those that a mesh axis runs over, the one named last changes fastest.
Arguments:
- latents: bfloat16 [1024, 1024], P('expert'), may hold values from -6 to 6
- out_grad: bfloat16 [1024, 1024], P('expert'), may hold values from -6 to 6
- routes: int32 [1024, 8], P('expert'), may hold values from 0 to 63, all different within a row; in each aligned block of 128 rows (0 to 127, 128 to 255, ...) at most 32 rows name the same one
- route_weights: float32 [1024, 8], P('expert'), may hold values from 0.1 to 1
- gate_weight: bfloat16 [64, 1024, 768], P('expert', None, 'dp'), may hold values from -0.1875 to 0.1875
- up_weight: bfloat16 [64, 1024, 768], P('expert', None, 'dp'), may hold values from -0.1875 to 0.1875
- down_weight: bfloat16 [64, 1024, 768], P('expert', None, 'dp'), may hold values from -0.21875 to 0.21875
Outputs:
- mixed: bfloat16 [1024, 1024], P('expert')
- latent_grad: bfloat16 [1024, 1024], P('expert')
- weight_grad: float32 [1024, 8], P('expert')
Inputs may be any that keep to these rules, and one draw needn't show every extreme that they name: `routes`: each row names 8 different experts. Among the rows of one index of expert no expert is named more than 32 times, and in every draw some index's rows name some expert exactly 32 times.
All inputs are finite; a program needn't handle non-finite values.
Results may differ from a plain program's by a relative error of at most 0.0064.
Values may be sent and summed in bfloat16 or wider, within the bound.
A program may use at most 128 MiB of HBM per device.

v0:
```python
import jax
import jax.numpy as jnp
from jax import lax
from jax.sharding import PartitionSpec as P

CAP = 32


def expert_terms(pieces, slot_in, slot_cot):
    gate_piece, up_piece, down_piece = pieces
    gate_act = jnp.einsum("erl,elh->erh", slot_in, gate_piece, preferred_element_type=jnp.float32)
    up_act = jnp.einsum("erl,elh->erh", slot_in, up_piece, preferred_element_type=jnp.float32)
    sigmoid_gate = jax.nn.sigmoid(gate_act)
    silu_gate = gate_act * sigmoid_gate
    hidden = (silu_gate * up_act).astype(jnp.bfloat16)
    mixed_sum = jnp.einsum("erh,elh->erl", hidden, down_piece, preferred_element_type=jnp.float32)
    grad_hidden = jnp.einsum(
        "erl,elh->erh", slot_cot, down_piece, preferred_element_type=jnp.float32
    )
    slope = sigmoid_gate * (1.0 + gate_act * (1.0 - sigmoid_gate))
    grad_gate = (grad_hidden * up_act * slope).astype(jnp.bfloat16)
    grad_up = (grad_hidden * silu_gate).astype(jnp.bfloat16)
    grad_sum = jnp.einsum("erh,elh->erl", grad_gate, gate_piece, preferred_element_type=jnp.float32)
    grad_sum = grad_sum + jnp.einsum(
        "erh,elh->erl", grad_up, up_piece, preferred_element_type=jnp.float32
    )
    return (mixed_sum, grad_sum)


def local(latents, out_grad, routes, route_weights, gate_weight, up_weight, down_weight):
    token_count, features = latents.shape
    top_count = routes.shape[1]
    local_experts = gate_weight.shape[0]
    groups = lax.axis_size("expert")
    experts = local_experts * groups
    share = CAP // lax.axis_size("dp")
    my_share = lax.axis_index("dp")
    pair_count = token_count * top_count
    routes_flat = routes.reshape(pair_count)
    onehot = (routes_flat[:, None] == jnp.arange(experts, dtype=jnp.int32)[None, :]).astype(
        jnp.int32
    )
    before = jnp.cumsum(onehot, axis=0) - onehot
    position = jnp.sum(before * onehot, axis=1)
    served = position // share == my_share
    spare_row = experts * share
    target = jnp.where(served, routes_flat * share + position - my_share * share, spare_row)
    pair_ids = jnp.arange(pair_count, dtype=jnp.int32)
    owners = pair_ids // top_count
    columns = pair_ids % top_count
    weights_flat = route_weights.reshape(pair_count)
    slot_token = (
        jnp.full((spare_row + 1,), token_count, jnp.int32).at[target].set(owners)[:spare_row]
    )
    slot_column = jnp.zeros((spare_row + 1,), jnp.int32).at[target].set(columns)[:spare_row]
    slot_weight = jnp.zeros((spare_row + 1,), jnp.float32).at[target].set(weights_flat)[:spare_row]
    valid = slot_token < token_count
    valid_wide = valid.astype(jnp.float32)
    slot_weight = slot_weight * valid_wide
    clipped = jnp.minimum(slot_token, token_count - 1)
    slot_upstream = out_grad[clipped].astype(jnp.float32)
    send_in = jnp.where(valid[:, None], latents[clipped], jnp.zeros((), jnp.bfloat16))
    send_cot = (slot_weight[:, None] * slot_upstream).astype(jnp.bfloat16)
    send_in = send_in.reshape(groups, local_experts * share, features)
    send_cot = send_cot.reshape(groups, local_experts * share, features)
    recv_in, recv_cot = (
        lax.all_to_all(send_in, "expert", split_axis=0, concat_axis=0, tiled=True),
        lax.all_to_all(send_cot, "expert", split_axis=0, concat_axis=0, tiled=True),
    )
    slot_count = groups * share
    slot_in = (
        recv_in.reshape(groups, local_experts, share, features)
        .transpose(1, 0, 2, 3)
        .reshape(local_experts, slot_count, features)
    )
    slot_cot = (
        recv_cot.reshape(groups, local_experts, share, features)
        .transpose(1, 0, 2, 3)
        .reshape(local_experts, slot_count, features)
    )
    whole_gate, whole_up, whole_down = (
        lax.all_gather(gate_weight, "dp", axis=2, tiled=True),
        lax.all_gather(up_weight, "dp", axis=2, tiled=True),
        lax.all_gather(down_weight, "dp", axis=2, tiled=True),
    )
    mixed_slots, grad_slots = expert_terms((whole_gate, whole_up, whole_down), slot_in, slot_cot)
    back_mix = (
        mixed_slots.astype(jnp.bfloat16)
        .reshape(local_experts, groups, share, features)
        .transpose(1, 0, 2, 3)
        .reshape(groups, local_experts * share, features)
    )
    back_grad = (
        grad_slots.astype(jnp.bfloat16)
        .reshape(local_experts, groups, share, features)
        .transpose(1, 0, 2, 3)
        .reshape(groups, local_experts * share, features)
    )
    got_mix, got_grad = (
        lax.all_to_all(back_mix, "expert", split_axis=0, concat_axis=0, tiled=True),
        lax.all_to_all(back_grad, "expert", split_axis=0, concat_axis=0, tiled=True),
    )
    slot_out = got_mix.reshape(spare_row, features).astype(jnp.float32)
    slot_grad = got_grad.reshape(spare_row, features).astype(jnp.float32)
    mixed_part = (
        jnp.zeros((token_count, features), jnp.float32)
        .at[clipped]
        .add(slot_weight[:, None] * slot_out)
    )
    grad_part = (
        jnp.zeros((token_count, features), jnp.float32)
        .at[clipped]
        .add(valid_wide[:, None] * slot_grad)
    )
    slot_score = valid_wide * jnp.sum(slot_upstream * slot_out, axis=1)
    score_part = (
        jnp.zeros((token_count, top_count), jnp.float32).at[clipped, slot_column].add(slot_score)
    )
    mixed_total, grad_total, score_total = lax.psum((mixed_part, grad_part, score_part), "dp")
    return (mixed_total.astype(jnp.bfloat16), grad_total.astype(jnp.bfloat16), score_total)


def solution(mesh):
    placed = (
        P("expert", None),
        P("expert", None),
        P("expert", None),
        P("expert", None),
        P("expert", None, "dp"),
        P("expert", None, "dp"),
        P("expert", None, "dp"),
    )
    return jax.shard_map(
        local,
        mesh=mesh,
        in_specs=placed,
        out_specs=(P("expert", None), P("expert", None), P("expert", None)),
        check_vma=False,
    )
```

profile of v0, /device:TPU:0, one launch (start us, length us, event | category | flops | bytes accessed | tf_op | source)
XLA Modules:
  0.0 566.9 jit_solution(11819924167566891340)
XLA Ops:
  10.0 18.0 %reduce-window.6 = s32[64,8,128]{2,1,0:T(8,128)S(1)} reduce-window(s32[64,8,128]{2,1,0:T(8,128)S(1)} %fusion.26, s32[]{:T(128)} %constant.61.clone.1), window={size=1x1x128 pad=0_0x0_0x127_0}, to_apply=%region_0.0 | reduce-window | flops 8323072 | bytes 524292 | tf_op jit(solution)/shard_map/reduce-window
  28.6 4.3 scatter_custom_fusion
  33.1 2.1 gather_fusion
  35.3 32.7 %all_to_all.20 = bf16[8,64,1024]{2,1,0:T(8,128)(2,1)S(1)} all-to-all(bf16[8,64,1024]{2,1,0:T(8,128)(2,1)S(1)} %broadcast_select_fusion), channel_id=1, replica_groups=mesh['dp'=4,'expert'=8] {'expert'}, dimensions={0} | all-to-all | bytes 2097152 | tf_op jit(solution)/shard_map/all_to_all | solution.py:67
  68.0 67.2 %all-gather.4.cloned.1.call-done = bf16[8,1024,768]{1,2,0:T(8,128)(2,1)} async-done(((bf16[8,1024,192]{1,2,0:T(8,128)(2,1)}), bf16[8,1024,768]{1,2,0:T(8,128)(2,1)}) %all-gather.4.cloned.1.call-update) | async-done | bytes 12582928 | tf_op jit(solution)/shard_map/all_gather | solution.py:82
  135.2 8.5 %fusion.10 = f32[8,64,768]{2,1,0:T(8,128)S(1)} fusion(bf16[8,1024,768]{1,2,0:T(8,128)(2,1)} %all-gather.4.cloned.1.call-done, bf16[8,64,1024]{2,1,0:T(8,128)(2,1)S(1)} %all_to_all.20), kind=kOutput, calls=%fused_computation.28 | convolution fusion | flops 805306368 | bytes 15204352 | tf_op jit(solution)/shard_map/erl,elh->erh/dot_general | solution.py:11
  143.7 115.9 %all-gather.6.cloned.1.call-done = bf16[8,1024,768]{1,2,0:T(8,128)(2,1)} async-done(((bf16[8,1024,192]{1,2,0:T(8,128)(2,1)}), bf16[8,1024,768]{1,2,0:T(8,128)(2,1)}) %all-gather.6.cloned.1.call-update) | async-done | bytes 12582928 | tf_op jit(solution)/shard_map/all_gather | solution.py:83
  259.6 8.8 %fusion.8 = f32[8,64,768]{2,1,0:T(8,128)S(1)} fusion(bf16[8,1024,768]{1,2,0:T(8,128)(2,1)} %all-gather.6.cloned.1.call-done, bf16[8,64,1024]{2,1,0:T(8,128)(2,1)} %copy-done.3), kind=kOutput, calls=%fused_computation.26 | convolution fusion | flops 805306368 | bytes 15204352 | tf_op jit(solution)/shard_map/erl,elh->erh/dot_general | solution.py:12
  268.4 115.6 %all-gather.8.cloned.1.call-done = bf16[8,1024,768]{1,2,0:T(8,128)(2,1)} async-done(((bf16[8,1024,192]{1,2,0:T(8,128)(2,1)}), bf16[8,1024,768]{1,2,0:T(8,128)(2,1)}) %all-gather.8.cloned.1.call-update) | async-done | bytes 12582928 | tf_op jit(solution)/shard_map/all_gather | solution.py:84
  384.0 6.9 %fusion.4 = bf16[8,8,8,1024]{3,2,1,0:T(8,128)(2,1)S(1)} fusion(bf16[8,1024,768]{1,2,0:T(8,128)(2,1)} %all-gather.8.cloned.1.call-done, f32[8,64,768]{2,1,0:T(8,128)S(1)} %fusion.8, f32[8,64,768]{2,1,0:T(8,128)S(1)} %fusion.10), kind=kOutput, calls=%fused_computation.22 | convolution fusion | flops 808189952 | bytes 16777216 | tf_op jit(solution)/shard_map/erh,elh->erl/dot_general | solution.py:16
  391.9 4.6 all-to-all-start.1
  396.7 2.8 gather_fusion.1
  399.5 4.3 scatter_custom_fusion.1
  403.8 19.4 %all-to-all-done.1 = bf16[8,64,1024]{2,1,0:T(8,128)(2,1)} async-done(((bf16[8,64,1024]{2,1,0:T(8,128)(2,1)}), bf16[8,64,1024]{2,1,0:T(8,128)(2,1)}, u32[]{:S(2)}, u32[]{:S(2)}) %all-to-all-start.1) | async-done | bytes 1048608 | tf_op jit(solution)/shard_map/all_to_all | solution.py:100
  426.7 29.0 %all_to_all.21 = bf16[8,64,1024]{2,1,0:T(8,128)(2,1)S(1)} all-to-all(bf16[8,64,1024]{2,1,0:T(8,128)(2,1)S(1)} %fusion), channel_id=1, replica_groups=mesh['dp'=4,'expert'=8] {'expert'}, dimensions={0} | all-to-all | bytes 2097152 | tf_op jit(solution)/shard_map/all_to_all | solution.py:68
  455.8 8.6 %fusion.6 = f32[8,64,768]{2,1,0:T(8,128)S(1)} fusion(bf16[8,1024,768]{1,2,0:T(8,128)(2,1)} %all-gather.8.cloned.1.call-done, bf16[8,64,1024]{2,1,0:T(8,128)(2,1)S(1)} %all_to_all.21), kind=kOutput, calls=%fused_computation.24 | convolution fusion | flops 805306368 | bytes 15204352 | tf_op jit(solution)/shard_map/erl,elh->erh/dot_general | solution.py:17
  464.4 7.1 %fusion.16 = f32[8,64,1024]{2,1,0:T(8,128)S(1)} fusion(bf16[8,1024,768]{1,2,0:T(8,128)(2,1)} %all-gather.4.cloned.1.call-done, f32[8,64,768]{2,1,0:T(8,128)S(1)} %fusion.10, f32[8,64,768]{2,1,0:T(8,128)S(1)} %fusion.6, f32[8,64,768]{2,1,0:T(8,128)S(1)} %fusion.8), kind=kOutput, calls=%fused_computation.37 | convolution fusion | flops 809238528 | bytes 19398656 | tf_op jit(solution)/shard_map/erh,elh->erl/dot_general | solution.py:23
  471.6 2.4 fusion.5
  475.0 3.6 all-to-all-start.3
  478.6 4.5 scatter_custom_fusion.4
  484.6 5.5 scatter_custom_fusion.2
  490.1 22.1 %scatter_fusion = f32[128,8]{0,1:T(8,128)S(1)} fusion(f32[128,8]{0,1:T(8,128)S(1)} %broadcast_in_dim.52, s32[512]{0:T(512)S(1)} %bitcast.79, f32[512]{0:T(512)S(1)} %get-tuple-element.10), kind=kCustom, calls=%fused_computation.7 | custom fusion | flops 512 | bytes 10240 | tf_op jit(solution)/shard_map/scatter-add | solution.py:117
  512.2 5.0 scatter_custom_fusion.3
  517.2 43.2 %all-reduce.2 = (bf16[128,1024]{1,0:T(8,128)(2,1)}, bf16[128,1024]{1,0:T(8,128)(2,1)}, f32[128,8]{0,1:T(8,128)}) all-reduce(f32[128,1024]{1,0:T(8,128)S(1)} %copy-done.4, f32[128,1024]{1,0:T(8,128)S(1)} %scatter_custom_fusion.3, f32[128,8]{0,1:T(8,128)S(1)} %scatter_fusion), channel_id=1, replica_groups=mesh['dp'=4,'expert'=8] {'dp'}, use_global_device_ids=true, to_apply=%region_6.7 | all-reduce | flops 263168 | bytes 1581056 | tf_op jit(solution)/shard_map/psum | solution.py:119
  (64 shorter events, 10.9 us)
Async XLA Ops:
  7.2 25.9 %copy-start = (bf16[128,1024]{1,0:T(8,128)(2,1)S(1)}, bf16[128,1024]{1,0:T(8,128)(2,1)}, u32[]{:S(2)}) copy-start(bf16[128,1024]{1,0:T(8,128)(2,1)} %param.7) | copy-start | bytes 786436
  7.2 128.0 %all-gather.4.cloned.1.call-start = ((), (), s32[]{:S(2)}) async-start(), calls=%async_computation.4 | async-start | bytes 15728640 | tf_op jit(solution)/shard_map/all_gather | solution.py:82
  7.9 251.7 %all-gather.6.cloned.1.call-start = ((), (), s32[]{:S(2)}) async-start(), calls=%async_computation.5 | async-start | bytes 15728640 | tf_op jit(solution)/shard_map/all_gather | solution.py:83
  8.7 0.8 copy-start.5
  8.7 375.3 %all-gather.8.cloned.1.call-start = ((), (), s32[]{:S(2)}) async-start(), calls=%async_computation.6 | async-start | bytes 15728640 | tf_op jit(solution)/shard_map/all_gather | solution.py:84
  68.0 75.7 %copy-start.3 = (bf16[8,64,1024]{2,1,0:T(8,128)(2,1)}, bf16[8,64,1024]{2,1,0:T(8,128)(2,1)S(1)}, u32[]{:S(2)}) copy-start(bf16[8,64,1024]{2,1,0:T(8,128)(2,1)S(1)} %all_to_all.20) | copy-start | bytes 3145732
  390.8 5.7 %copy-start.6 = (f32[128,8]{0,1:T(8,128)S(1)}, f32[128,8]{0,1:T(8,128)}, u32[]{:S(2)}) copy-start(f32[128,8]{0,1:T(8,128)} %param.10) | copy-start | bytes 12292
  390.9 5.9 %copy-start.2 = (bf16[128,1024]{1,0:T(8,128)(2,1)S(1)}, bf16[128,1024]{1,0:T(8,128)(2,1)}, u32[]{:S(2)}) copy-start(bf16[128,1024]{1,0:T(8,128)(2,1)} %param.8) | copy-start | bytes 786436
  391.9 31.3 %all-to-all-start.1 = ((bf16[8,64,1024]{2,1,0:T(8,128)(2,1)}), bf16[8,64,1024]{2,1,0:T(8,128)(2,1)}, u32[]{:S(2)}, u32[]{:S(2)}) async-start(bf16[8,64,1024]{2,1,0:T(8,128)(2,1)} %bitcast.83), calls=%async_computation.1 | async-start | bytes 2097152 | tf_op jit(solution)/shard_map/all_to_all | solution.py:100
  455.8 15.8 %slice-start = ((s8[12582912]{0:T(1024)(128)(4,1)}), s8[4194304]{0:T(1024)(128)(4,1)S(1)}, s32[]{:S(2)}) async-start(s8[12582912]{0:T(1024)(128)(4,1)} %bitcast.77), calls=%async_computation.7 | async-start | bytes 8388608
  455.8 15.8 %slice-start.1 = ((s8[12582912]{0:T(1024)(128)(4,1)}), s8[4194304]{0:T(1024)(128)(4,1)S(1)}, s32[]{:S(2)}) async-start(s8[12582912]{0:T(1024)(128)(4,1)} %bitcast.77), calls=%async_computation.8 | async-start | bytes 8388608
  464.4 7.2 %slice-start.2 = ((s8[12582912]{0:T(1024)(128)(4,1)}), s8[4194304]{0:T(1024)(128)(4,1)S(1)}, s32[]{:S(2)}) async-start(s8[12582912]{0:T(1024)(128)(4,1)} %bitcast.77), calls=%async_computation.9 | async-start | bytes 8388608
  475.0 37.2 %all-to-all-start.3 = ((bf16[8,64,1024]{2,1,0:T(8,128)(2,1)}), bf16[8,64,1024]{2,1,0:T(8,128)(2,1)S(1)}, u32[]{:S(2)}, u32[]{:S(2)}) async-start(bf16[8,64,1024]{2,1,0:T(8,128)(2,1)} %bitcast.72), calls=%async_computation.3 | async-start | bytes 2097152 | tf_op jit(solution)/shard_map/all_to_all | solution.py:101
  490.1 27.1 %copy-start.4 = (f32[128,1024]{1,0:T(8,128)S(1)}, f32[128,1024]{1,0:T(8,128)}, u32[]{:S(2)}) copy-start(f32[128,1024]{1,0:T(8,128)} %scatter_custom_fusion.2) | copy-start | bytes 1572868
  490.1 70.3 %copy-start.1 = (bf16[128,1024]{1,0:T(8,128)(2,1)S(1)}, bf16[128,1024]{1,0:T(8,128)(2,1)}, u32[]{:S(2)}) copy-start(bf16[128,1024]{1,0:T(8,128)(2,1)} %param.7) | copy-start | bytes 786436
Sparse Core Ops, SparseCore 0:
  9.9 125.2 all-gather.3
  137.0 122.5 all-gather.5
  261.4 122.5 all-gather.7
where the time goes:
time: 567 us
  waiting for transfers between devices  320 us (56%)
  blocking collectives  105 us (19%)
  other arithmetic  55.8 us (10%)
  matrix products  42.4 us (7%)
  local copies, waits for them, and re-layouts  21.5 us (4%)
  between operations  14.1 us (2%)
  starting transfers between devices  8.28 us (1%)
    all_gather x1, waiting for transfers between devices, local(): lax.all_gather(up_weight, 'dp', axis=2, tiled=True)  116 us
    all_gather x1, waiting for transfers between devices, local(): lax.all_gather(down_weight, 'dp', axis=2, tiled=True)  116 us
    all_gather x1, waiting for transfers between devices, local(): lax.all_gather(gate_weight, 'dp', axis=2, tiled=True)  67.2 us
    psum x1, blocking collectives, local(): lax.psum((mixed_part, grad_part, score_part), 'dp')  43.2 us
    all_to_all x1, blocking collectives, local(): lax.all_to_all(send_in, 'expert', split_axis=0, concat_axis=0, tiled=True)  32.7 us
    all_to_all x1, blocking collectives, local(): lax.all_to_all(send_cot, 'expert', split_axis=0, concat_axis=0, tiled=True)  29 us
    scatter-add x1, other arithmetic, local(): jnp.zeros((token_count, top_count), jnp.float32).at[clipped, slot_column]  22.1 us
    all_to_all x1, waiting for transfers between devices, local(): lax.all_to_all(back_mix, 'expert', split_axis=0, concat_axis=0, tiled=True)  19.4 us
  transfers between devices with their start and end apart: 5, of which 4 were waited for; matrix products, arithmetic and copies ran while one was open for 15% of the time, Pallas kernels for 0%

commit v1 on v0

v1 whole, which is shorter than its diff:
```python
import jax
import jax.numpy as jnp
from jax import lax
from jax.sharding import PartitionSpec as P


def local(latents, out_grad, routes, route_weights, gate_weight, up_weight, down_weight):
    features = latents.shape[1]
    local_experts = gate_weight.shape[0]
    groups = lax.axis_size("expert")
    experts = local_experts * groups
    me = lax.axis_index("expert")
    hot = routes[:, :, None] == jnp.arange(experts, dtype=jnp.int32)[None, None, :]
    table = jnp.sum(jnp.where(hot, route_weights[:, :, None], 0.0), axis=1)
    high = table.astype(jnp.bfloat16)
    low = (table - high.astype(jnp.float32)).astype(jnp.bfloat16)
    payload = jnp.concatenate([latents, out_grad, high, low], axis=1)
    got = lax.all_gather(payload, "expert", axis=0, tiled=True)
    tokens = got[:, :features]
    upstream = got[:, features : 2 * features]
    mine_high = lax.dynamic_slice_in_dim(got, 2 * features + me * local_experts, local_experts, 1)
    mine_low = lax.dynamic_slice_in_dim(
        got, 2 * features + experts + me * local_experts, local_experts, 1
    )
    weight = mine_high.astype(jnp.float32) + mine_low.astype(jnp.float32)
    weight = weight.T[:, :, None]
    gate_act = jnp.einsum("tl,elh->eth", tokens, gate_weight, preferred_element_type=jnp.float32)
    up_act = jnp.einsum("tl,elh->eth", tokens, up_weight, preferred_element_type=jnp.float32)
    back = jnp.einsum("tl,elh->eth", upstream, down_weight, preferred_element_type=jnp.float32)
    sig = jax.nn.sigmoid(gate_act)
    silu = gate_act * sig
    hidden = silu * up_act
    valid = (weight > 0).astype(jnp.float32)
    score = jnp.sum(hidden * back * valid, axis=2).T
    weighted = (hidden * weight).astype(jnp.bfloat16)
    back = back * weight
    slope = sig * (1.0 + gate_act * (1.0 - sig))
    grad_gate = (back * up_act * slope).astype(jnp.bfloat16)
    grad_up = (back * silu).astype(jnp.bfloat16)
    mixed = jnp.einsum("eth,elh->tl", weighted, down_weight, preferred_element_type=jnp.float32)
    grad = jnp.einsum("eth,elh->tl", grad_gate, gate_weight, preferred_element_type=jnp.float32)
    grad = grad + jnp.einsum("eth,elh->tl", grad_up, up_weight, preferred_element_type=jnp.float32)
    wide = jnp.zeros((got.shape[0], experts), jnp.float32)
    wide = lax.dynamic_update_slice_in_dim(wide, score, me * local_experts, 1)
    parts = jnp.concatenate([mixed, grad, wide], axis=1).astype(jnp.bfloat16)
    parts = parts.reshape(groups, latents.shape[0], parts.shape[1])
    moved = lax.all_to_all(parts, "expert", split_axis=0, concat_axis=0, tiled=True)
    summed = jnp.sum(moved.astype(jnp.float32), axis=0)
    total = lax.psum(summed, "dp")
    final = total[:, 2 * features :]
    weight_grad = jnp.sum(jnp.where(hot, final[:, None, :], 0.0), axis=2)
    return (
        total[:, :features].astype(jnp.bfloat16),
        total[:, features : 2 * features].astype(jnp.bfloat16),
        weight_grad,
    )


def solution(mesh):
    row = P("expert", None)
    cut = P("expert", None, "dp")
    return jax.shard_map(
        local,
        mesh=mesh,
        in_specs=(row, row, row, row, cut, cut, cut),
        out_specs=(row, row, row),
        check_vma=False,
    )
```

time: 567 us -> 282 us (0.50)
  waiting for transfers between devices: 320 us -> 105 us
  other arithmetic: 55.8 us -> 12.1 us
  starting transfers between devices: 8.28 us -> 0.08 us
  matrix products: 42.4 us -> 35.9 us
  local copies, waits for them, and re-layouts: 21.5 us -> 15 us
  blocking collectives: 105 us -> 99.3 us
    all_gather x3 -> x1, waiting for transfers between devices: 299 us -> 52.8 us  [local(): got = lax.all_gather(payload, 'expert', axis=0, tiled=True)]
    psum x0 -> x1, waiting for transfers between devices: none -> 52.1 us  [local(): total = lax.psum(summed, 'dp')]
    psum x1 -> x0, blocking collectives: 43.2 us -> none  [local(): lax.psum((mixed_part, grad_part, score_part), 'dp')]
    all_to_all x2 -> x1, blocking collectives: 61.7 us -> 99.3 us  [local(): lax.all_to_all(parts, 'expert', split_axis=0, concat_axis=0, tiled=True)]
    scatter-add x3 -> x0, other arithmetic: 32.5 us -> none  [the longest x1 22.1 us: local(): jnp.zeros((token_count, top_count), jnp.float32).at[clipped, slot_column]]
    dot_general x6 -> x3, matrix products: 42.4 us -> 22.7 us  [the longest x1 12 us: local(): jnp.einsum('eth,elh->tl', grad_gate, gate_weight, preferred_element_type=...]
    all_to_all x2 -> x0, waiting for transfers between devices: 19.4 us -> none  [the longest x1 19.4 us: local(): lax.all_to_all(back_mix, 'expert', split_axis=0, concat_axis=0, tiled=True)]
    another operation x3 -> x1, other arithmetic: 18.2 us -> 1.29 us
  transfers between devices with their start and end apart: 5 -> 2, of which waited for: 4 -> 2; matrix products, arithmetic and copies ran while one was open for 15% -> 0% of each run, Pallas kernels for 0% -> 0%
where the time goes in v1:
time: 282 us
  waiting for transfers between devices  105 us (37%)
  blocking collectives  99.3 us (35%)
  matrix products  35.9 us (13%)
  local copies, waits for them, and re-layouts  15 us (5%)
  between operations  14.2 us (5%)
  other arithmetic  12.1 us (4%)
    all_to_all x1, blocking collectives, local(): lax.all_to_all(parts, 'expert', split_axis=0, concat_axis=0, tiled=True)  99.3 us
    all_gather x1, waiting for transfers between devices, local(): got = lax.all_gather(payload, 'expert', axis=0, tiled=True)  52.8 us
    psum x1, waiting for transfers between devices, local(): total = lax.psum(summed, 'dp')  52.1 us
    unnamed x3, matrix products  13.2 us
    dot_general x1, matrix products, local(): jnp.einsum('eth,elh->tl', grad_gate, gate_weight, preferred_element_type=...  12 us
    concatenate x3, local copies, waits for them, and re-layouts, local(): parts = jnp.concatenate([mixed, grad, wide], axis=1).astype(jnp.bfloat16)  7.86 us
    dot_general x1, matrix products, local(): jnp.einsum('eth,elh->tl', grad_up, up_weight, preferred_element_type=jnp....  5.67 us
  transfers between devices with their start and end apart: 2, of which 2 were waited for; matrix products, arithmetic and copies ran while one was open for 0% of the time, Pallas kernels for 0%

profile of v1, /device:TPU:0, one launch (start us, length us, event | category | flops | bytes accessed | tf_op | source)
XLA Modules:
  0.0 281.5 jit_solution(12276514294076696499)
XLA Ops:
  7.2 0.9 select_reduce_fusion.1
  8.1 1.1 copy.47
  9.3 1.8 copy.46
  11.1 1.8 pad_maximum_fusion.1
  12.9 52.8 %all-gather.2.cloned.1.call-done = bf16[1024,2176]{0,1:T(8,128)(2,1)} async-done(((bf16[128,2176]{0,1:T(8,128)(2,1)}), bf16[1024,2176]{0,1:T(8,128)(2,1)}) %all-gather.2.cloned.1.call-update) | async-done | bytes 4456464 | tf_op jit(solution)/shard_map/all_gather | solution.py:18
  65.7 6.2 %fusion.8 = f32[1024,1536]{0,1:S(1)} fusion(bf16[1024,1536]{0,1:T(8,128)(2,1)} %bitcast.59, bf16[1024,2176]{0,1:T(8,128)(2,1)} %all-gather.2.cloned.1.call-done), kind=kOutput, calls=%fused_computation.17 | convolution fusion | flops 3221225472 | bytes 11534336
  72.0 3.5 %fusion.10 = f32[1024,1536]{0,1:S(1)} fusion(bf16[1024,1536]{0,1:T(8,128)(2,1)S(1)} %bitcast.60, bf16[1024,2176]{0,1:T(8,128)(2,1)S(1)} %copy-done.3), kind=kOutput, calls=%fused_computation.19 | convolution fusion | flops 3221225472 | bytes 11534336
  75.5 5.7 %fusion.3 = f32[1024,1024,1]{1,0,2:T(8,128)} fusion(bf16[8,1024,192]{1,2,0:T(8,128)(2,1)S(1)} %copy-done, f32[8,1024,192]{1,2,0:T(8,128)S(1)} %bitcast.47, f32[8,1024]{1,0:T(8,128)S(1)} %get-tuple-element.13, f32[8,1024,192]{1,2,0:T(8,128)S(1)} %bitcast.50), kind=kOutput, calls=%fused_computation.12 | convolution fusion | flops 3232235520 | bytes 19955712 | tf_op jit(solution)/shard_map/eth,elh->tl/dot_general | solution.py:42
  81.2 3.5 %fusion.12 = f32[1024,1536]{0,1:S(1)} fusion(bf16[1024,1536]{0,1:T(8,128)(2,1)S(1)} %bitcast.46, bf16[1024,2176]{0,1:T(8,128)(2,1)S(1)} %copy-done.3), kind=kOutput, calls=%fused_computation.21 | convolution fusion | flops 3221225472 | bytes 11534336
  84.7 5.1 %bitcast_convert_fusion = bf16[1024,1024]{1,0:T(8,128)(2,1)} fusion(bf16[8,1024,192]{1,2,0:T(8,128)(2,1)S(1)} %copy-done.4, f32[8,1024]{1,0:T(8,128)S(1)} %get-tuple-element.13, f32[8,1024,192]{1,2,0:T(8,128)S(1)} %bitcast.54, f32[8,1024,192]{1,2,0:T(8,128)S(1)} %bitcast.51), kind=kOutput, calls=%fused_computation.10 | convolution fusion | flops 3233284096 | bytes 17858560 | tf_op jit(solution)/shard_map/eth,elh->tl/dot_general | solution.py:40
  89.8 3.5 %multiply_reduce_fusion = bf16[8,1024]{1,0:T(8,128)(2,1)S(1)} fusion(f32[8,1024,192]{1,2,0:T(8,128)S(1)} %bitcast.48, f32[8,1024]{1,0:T(8,128)S(1)} %get-tuple-element.12, f32[8,1024,192]{1,2,0:T(8,128)S(1)} %bitcast.55, f32[8,1024,192]{1,2,0:T(8,128)S(1)} %bitcast.52), kind=kLoop, calls=%fused_computation.1 | loop fusion | flops 12574720 | bytes 18923520 | tf_op jit(solution)/shard_map/reduce_sum | solution.py:34
  93.4 12.0 %fusion.1 = bf16[1024,1024]{1,0:T(8,128)(2,1)} fusion(f32[1024,1024,1]{1,0,2:T(8,128)} %fusion.3, bf16[8,1024,192]{1,2,0:T(8,128)(2,1)} %param.11, f32[8,1024,192]{1,2,0:T(8,128)S(1)} %bitcast.53, f32[8,1024,192]{1,2,0:T(8,128)} %bitcast.56, f32[8,1024,192]{1,2,0:T(8,128)S(1)} %bitcast.49, f32[8,1024]{1,0:T(8,128)S(1)} %get-tuple-element.13), kind=kOutput, calls=%fused_computation.9 | convolution fusion | flops 3240624128 | bytes 28344320 | tf_op jit(solution)/shard_map/eth,elh->tl/dot_general | solution.py:41
  105.3 3.9 %copy.52 = bf16[8,128,1024]{1,2,0:T(8,128)(2,1)} copy(bf16[8,128,1024]{2,1,0:T(8,128)(2,1)} %bitcast.58) | data formatting | bytes 4194304 | tf_op jit(solution)/shard_map/concatenate | solution.py:45
  109.2 3.9 %copy.51 = bf16[8,128,1024]{1,2,0:T(8,128)(2,1)} copy(bf16[8,128,1024]{2,1,0:T(8,128)(2,1)} %bitcast.57) | data formatting | bytes 4194304 | tf_op jit(solution)/shard_map/concatenate | solution.py:45
  113.2 2.3 pad_maximum_fusion
  115.5 99.3 %all_to_all.5 = bf16[8,128,2112]{1,2,0:T(8,128)(2,1)S(1)} all-to-all(bf16[8,128,2112]{1,2,0:T(8,128)(2,1)S(1)} %pad_maximum_fusion), channel_id=1, replica_groups=mesh['dp'=4,'expert'=8] {'expert'}, dimensions={0} | all-to-all | bytes 8650752 | tf_op jit(solution)/shard_map/all_to_all | solution.py:47
  214.8 1.7 convert_reduce_fusion
  216.5 52.1 %all-reduce.2.cloned.1.call-done = f32[128,2112]{0,1:T(8,128)} async-done(((f32[128,2112]{0,1:T(8,128)}), f32[128,2112]{0,1:T(8,128)}) %all-reduce.2.cloned.1.call-update) | async-done | bytes 1081360 | tf_op jit(solution)/shard_map/psum | solution.py:49
  268.6 1.3 convert.19
  269.9 0.7 fusion.17
  270.6 1.8 copy.54
  272.4 0.8 copy.55
  273.3 0.8 slice.26
  274.0 0.6 select_reduce_fusion
  (21 shorter events, 0.2 us)
Async XLA Ops:
  7.2 68.3 %copy-start = (bf16[8,1024,192]{1,2,0:T(8,128)(2,1)S(1)}, bf16[8,1024,192]{1,2,0:T(8,128)(2,1)}, u32[]{:S(2)}) copy-start(bf16[8,1024,192]{1,2,0:T(8,128)(2,1)} %param.12) | copy-start | bytes 9437188
  7.2 58.5 %all-gather.2.cloned.1.call-start = ((), (), s32[]{:S(2)}) async-start(), calls=%async_computation.1 | async-start | bytes 5013504 | tf_op jit(solution)/shard_map/all_gather | solution.py:18
  12.9 255.7 %all-reduce.2.cloned.1.call-start = ((), (), s32[]{:S(2)}) async-start(), calls=%async_computation.2 | async-start | bytes 2162688 | tf_op jit(solution)/shard_map/psum | solution.py:49
  65.7 6.2 %copy-start.3 = (bf16[1024,2176]{0,1:T(8,128)(2,1)S(1)}, bf16[1024,2176]{0,1:T(8,128)(2,1)}, u32[]{:S(2)}) copy-start(bf16[1024,2176]{0,1:T(8,128)(2,1)} %all-gather.2.cloned.1.call-done) | copy-start | bytes 13369348
  65.7 6.2 %copy-start.5 = (bf16[8,1024,192]{1,2,0:T(8,128)(2,1)S(1)}, bf16[8,1024,192]{1,2,0:T(8,128)(2,1)}, u32[]{:S(2)}) copy-start(bf16[8,1024,192]{1,2,0:T(8,128)(2,1)} %param.11) | copy-start | bytes 9437188
  81.2 3.6 %copy-start.4 = (bf16[8,1024,192]{1,2,0:T(8,128)(2,1)S(1)}, bf16[8,1024,192]{1,2,0:T(8,128)(2,1)}, u32[]{:S(2)}) copy-start(bf16[8,1024,192]{1,2,0:T(8,128)(2,1)} %param.13) | copy-start | bytes 9437188
  84.7 5.1 %copy-start.1 = (f32[1024,1536]{0,1}, f32[1024,1536]{0,1:S(1)}, u32[]{:S(2)}) copy-start(f32[1024,1536]{0,1:S(1)} %fusion.12) | copy-start | bytes 18874372
  214.8 59.2 %copy-start.2 = (s32[128,8]{0,1:T(8,128)S(1)}, s32[128,8]{0,1:T(8,128)}, u32[]{:S(2)}) copy-start(s32[128,8]{0,1:T(8,128)} %param.9) | copy-start | bytes 12292
Sparse Core Ops, SparseCore 0:
  13.0 52.6 all-gather.1
  216.6 51.9 all-reduce.1

commit v2 on v1

--- a/solution.py
+++ b/solution.py
@@ -1,7 +1,187 @@
+import functools
 import jax
 import jax.numpy as jnp
 from jax import lax
+from jax.experimental import pallas as pl
+from jax.experimental.pallas import tpu as pltpu
 from jax.sharding import PartitionSpec as P
+
+MESH = pl.DeviceIdType.MESH
+WHOLE_BYTES = 8 << 20
+
+
+def place(dp_count, z_count):
+    d = lax.axis_index("dp")
+    e = lax.axis_index("expert")
+    z = e // 2
+    c = e - 2 * z
+    partner = (d, 2 * z + 1 - c)
+    dp_to = [(lax.rem(d + k, dp_count), e) for k in range(dp_count)]
+    dp_from = [lax.rem(d + dp_count - k, dp_count) for k in range(dp_count)]
+    z_to = [lax.rem(z + j, z_count) for j in range(z_count)]
+    z_from = [lax.rem(z + z_count - j, z_count) for j in range(z_count)]
+    return d, z, c, partner, dp_to, dp_from, z_to, z_from
+
+
+def greet(d, c, partner, dp_to, z_to):
+    barrier = pltpu.get_barrier_semaphore()
+    peers = [partner] + dp_to[1:] + [(d, 2 * zt + c) for zt in z_to[1:]]
+    for peer in peers:
+        pl.semaphore_signal(barrier, inc=1, device_id=peer, device_id_type=MESH)
+    pl.semaphore_wait(barrier, len(peers))
+
+
+def push(src, dst, send_sem, recv_sem, peer):
+    return pltpu.make_async_remote_copy(
+        src_ref=src,
+        dst_ref=dst,
+        send_sem=send_sem,
+        recv_sem=recv_sem,
+        device_id=peer,
+        device_id_type=MESH,
+    )
+
+
+def gather_kernel(dp_count, z_count, own, out, local_sem, core_s, core_r, z_s, z_r, dp_s, dp_r):
+    d, z, c, partner, dp_to, dp_from, z_to, z_from = place(dp_count, z_count)
+    greet(d, c, partner, dp_to, z_to)
+    sent = []
+    for j in range(1, z_count):
+        copy = push(own.at[d], out.at[z, c, d], z_s.at[j], z_r.at[j], (d, 2 * z_to[j] + c))
+        copy.start()
+        sent.append(copy)
+    pair = push(own, out.at[z, c], core_s.at[0], core_r.at[0], partner)
+    pair.start()
+    sent.append(pair)
+    keep = pltpu.make_async_copy(own, out.at[z, c], local_sem)
+    keep.start()
+    for j in range(1, z_count):
+        zs = z_from[j]
+        mine = out.at[zs, c, d]
+        push(mine, mine, z_s.at[j], z_r.at[j], partner).wait_recv()
+        for k in range(1, dp_count):
+            copy = push(mine, mine, dp_s.at[j, k], dp_r.at[j, k], dp_to[k])
+            copy.start()
+            sent.append(copy)
+    for j in range(1, z_count):
+        zs = z_from[j]
+        for k in range(1, dp_count):
+            theirs = out.at[zs, c, dp_from[k]]
+            push(theirs, theirs, dp_s.at[j, k], dp_r.at[j, k], partner).wait_recv()
+        whole = out.at[zs, c]
+        copy = push(whole, whole, core_s.at[j], core_r.at[j], partner)
+        copy.start()
+        sent.append(copy)
+    keep.wait()
+    for j in range(z_count):
+        other = out.at[z_from[j], 1 - c]
+        push(other, other, core_s.at[j], core_r.at[j], partner).wait_recv()
+    for copy in sent:
+        copy.wait_send()
+
+
+def reduce_kernel(
+    dp_count, z_count, parts, out, half, quarter, core_in, dp_in, z_in,
+    core_s, core_r, dp_s, dp_r, z_s, z_r, end_s, end_r,
+):
+    d, z, c, partner, dp_to, dp_from, z_to, z_from = place(dp_count, z_count)
+    greet(d, c, partner, dp_to, z_to)
+    order = list(range(1, z_count)) + [0]
+    sent = []
+    for j in order:
+        copy = push(
+            parts.at[z_to[j], 1 - c], core_in.at[j], core_s.at[j], core_r.at[j], partner
+        )
+        copy.start()
+        sent.append(copy)
+    for j in order:
+        push(core_in.at[j], core_in.at[j], core_s.at[j], core_r.at[j], partner).wait_recv()
+        for k in list(range(1, dp_count)) + [0]:
+            to = dp_to[k][0]
+            half[j, k] = (
+                parts[z_to[j], c, to].astype(jnp.float32) + core_in[j, to].astype(jnp.float32)
+            ).astype(half.dtype)
+            if k > 0:
+                copy = push(
+                    half.at[j, k], dp_in.at[j, k], dp_s.at[j, k], dp_r.at[j, k], dp_to[k]
+                )
+                copy.start()
+                sent.append(copy)
+    for j in order:
+        total = half[j, 0].astype(jnp.float32)
+        for k in range(1, dp_count):
+            slot = dp_in.at[j, k]
+            push(slot, slot, dp_s.at[j, k], dp_r.at[j, k], partner).wait_recv()
+            total = total + dp_in[j, k].astype(jnp.float32)
+        if j > 0:
+            quarter[j] = total.astype(quarter.dtype)
+            copy = push(
+                quarter.at[j], z_in.at[j], z_s.at[j], z_r.at[j], (d, 2 * z_to[j] + c)
+            )
+            copy.start()
+            sent.append(copy)
+    for j in range(1, z_count):
+        push(z_in.at[j], z_in.at[j], z_s.at[j], z_r.at[j], partner).wait_recv()
+        total = total + z_in[j].astype(jnp.float32)
+    out[d] = total.astype(out.dtype)
+    for k in range(1, dp_count):
+        copy = push(out.at[d], out.at[d], end_s.at[k], end_r.at[k], dp_to[k])
+        copy.start()
+        sent.append(copy)
+    for k in range(1, dp_count):
+        theirs = out.at[dp_from[k]]
+        push(theirs, theirs, end_s.at[k], end_r.at[k], partner).wait_recv()
+    for copy in sent:
+        copy.wait_send()
+
+
+def gather_rows(payload, dp_count, groups):
+    rows, width = payload.shape
+    z_count = groups // 2
+    quarter = rows // dp_count
+    dma = pltpu.SemaphoreType.DMA
+    out = pl.pallas_call(
+        functools.partial(gather_kernel, dp_count, z_count),
+        out_shape=jax.ShapeDtypeStruct((z_count, 2, dp_count, quarter, width), payload.dtype),
+        in_specs=[pl.BlockSpec(memory_space=pltpu.VMEM)],
+        out_specs=pl.BlockSpec(memory_space=pltpu.VMEM),
+        scratch_shapes=[dma]
+        + [dma((z_count,))] * 4
+        + [dma((z_count, dp_count))] * 2,
+        compiler_params=pltpu.CompilerParams(
+            collective_id=0, has_side_effects=True, vmem_limit_bytes=32 << 20
+        ),
+    )(payload.reshape(dp_count, quarter, width))
+    return out.reshape(groups * rows, width)
+
+
+def reduce_rows(parts, dp_count, groups):
+    width = parts.shape[1]
+    z_count = groups // 2
+    quarter = parts.shape[0] // groups // dp_count
+    dma = pltpu.SemaphoreType.DMA
+    kind = parts.dtype
+    out = pl.pallas_call(
+        functools.partial(reduce_kernel, dp_count, z_count),
+        out_shape=jax.ShapeDtypeStruct((dp_count, quarter, width), kind),
+        in_specs=[pl.BlockSpec(memory_space=pltpu.VMEM)],
+        out_specs=pl.BlockSpec(memory_space=pltpu.VMEM),
+        scratch_shapes=[
+            pltpu.VMEM((z_count, dp_count, quarter, width), kind),
+            pltpu.VMEM((z_count, quarter, width), kind),
+            pltpu.VMEM((z_count, dp_count, quarter, width), kind),
+            pltpu.VMEM((z_count, dp_count, quarter, width), kind),
+            pltpu.VMEM((z_count, quarter, width), kind),
+        ]
+        + [dma((z_count,))] * 2
+        + [dma((z_count, dp_count))] * 2
+        + [dma((z_count,))] * 2
+        + [dma((dp_count,))] * 2,
+        compiler_params=pltpu.CompilerParams(
+            collective_id=1, has_side_effects=True, vmem_limit_bytes=48 << 20
+        ),
+    )(parts.reshape(z_count, 2, dp_count, quarter, width))
+    return out.reshape(dp_count * quarter, width)
 
 
 def local(latents, out_grad, routes, route_weights, gate_weight, up_weight, down_weight):
@@ -15,7 +195,13 @@
     high = table.astype(jnp.bfloat16)
     low = (table - high.astype(jnp.float32)).astype(jnp.bfloat16)
     payload = jnp.concatenate([latents, out_grad, high, low], axis=1)
-    got = lax.all_gather(payload, "expert", axis=0, tiled=True)
+    dp_count = lax.axis_size("dp")
+    rows = latents.shape[0]
+    fits = rows % (16 * dp_count) == 0 and groups * payload.size * 2 <= WHOLE_BYTES
+    if fits:
+        got = gather_rows(payload, dp_count, groups)
+    else:
+        got = lax.all_gather(payload, "expert", axis=0, tiled=True)
     tokens = got[:, :features]
     upstream = got[:, features : 2 * features]
     mine_high = lax.dynamic_slice_in_dim(got, 2 * features + me * local_experts, local_experts, 1)
@@ -40,14 +226,16 @@
     mixed = jnp.einsum("eth,elh->tl", weighted, down_weight, preferred_element_type=jnp.float32)
     grad = jnp.einsum("eth,elh->tl", grad_gate, gate_weight, preferred_element_type=jnp.float32)
     grad = grad + jnp.einsum("eth,elh->tl", grad_up, up_weight, preferred_element_type=jnp.float32)
-    wide = jnp.zeros((got.shape[0], experts), jnp.float32)
+    wide = jnp.zeros((got.shape[0], 2 * experts), jnp.float32)
     wide = lax.dynamic_update_slice_in_dim(wide, score, me * local_experts, 1)
     parts = jnp.concatenate([mixed, grad, wide], axis=1).astype(jnp.bfloat16)
-    parts = parts.reshape(groups, latents.shape[0], parts.shape[1])
-    moved = lax.all_to_all(parts, "expert", split_axis=0, concat_axis=0, tiled=True)
-    summed = jnp.sum(moved.astype(jnp.float32), axis=0)
-    total = lax.psum(summed, "dp")
-    final = total[:, 2 * features :]
+    if fits:
+        total = reduce_rows(parts, dp_count, groups)
+    else:
+        parts = parts.reshape(groups, rows, parts.shape[1])
+        moved = lax.all_to_all(parts, "expert", split_axis=0, concat_axis=0, tiled=True)
+        total = lax.psum(jnp.sum(moved.astype(jnp.float32), axis=0), "dp")
+    final = total[:, 2 * features : 2 * features + experts].astype(jnp.float32)
     weight_grad = jnp.sum(jnp.where(hot, final[:, None, :], 0.0), axis=2)
     return (
         total[:, :features].astype(jnp.bfloat16),

time: 282 us -> 141 us (0.50)
  waiting for transfers between devices: 105 us -> 0 us
  blocking collectives: 99.3 us -> 0 us
  Pallas kernels: 0 us -> 73.6 us
  matrix products: 35.9 us -> 49.7 us
  between operations: 14.2 us -> 0.87 us
  other arithmetic: 12.1 us -> 5.34 us
  local copies, waits for them, and re-layouts: 15 us -> 10.8 us
    all_to_all x1 -> x0, blocking collectives: 99.3 us -> none  [local(): lax.all_to_all(parts, 'expert', split_axis=0, concat_axis=0, tiled=True)]
    pallas_call x0 -> x2, Pallas kernels: none -> 73.6 us  [the longest x1 42.2 us: reduce_rows(): pl.pallas_call(functools.partial(reduce_kernel, dp_count, z_count), out_s...]
    all_gather x1 -> x0, waiting for transfers between devices: 52.8 us -> none  [local(): got = lax.all_gather(payload, 'expert', axis=0, tiled=True)]
    psum x1 -> x0, waiting for transfers between devices: 52.1 us -> none  [local(): total = lax.psum(summed, 'dp')]
    unnamed x3, matrix products: 13.2 us -> 21 us
    concatenate x3 -> x1, local copies, waits for them, and re-layouts: 7.86 us -> 1.9 us  [local(): payload = jnp.concatenate([latents, out_grad, high, low], axis=1)]
    dot_general x1, matrix products: 5.67 us -> 10.4 us  [local(): jnp.einsum('eth,elh->tl', grad_up, up_weight, preferred_element_type=jnp....]
    unnamed x16 -> x23, local copies, waits for them, and re-layouts: 5.59 us -> 2.35 us
  transfers between devices with their start and end apart: 2 -> 0, of which waited for: 2 -> 0; matrix products, arithmetic and copies ran while one was open for 0% -> 0% of each run, Pallas kernels for 0% -> 0%
where the time goes in v2:
time: 141 us; the launch traced here: 140 us
  Pallas kernels  73.6 us (52%)
  matrix products  49.7 us (35%)
  local copies, waits for them, and re-layouts  10.8 us (8%)
  other arithmetic  5.34 us (4%)
    pallas_call x1, Pallas kernels, reduce_rows(): pl.pallas_call(functools.partial(reduce_kernel, dp_count, z_count), out_s...  42.2 us
    pallas_call x1, Pallas kernels, gather_rows(): pl.pallas_call(functools.partial(gather_kernel, dp_count, z_count), out_s...  31.4 us
    unnamed x3, matrix products  21 us
    dot_general x1, matrix products, local(): jnp.einsum('eth,elh->tl', grad_gate, gate_weight, preferred_element_type=...  10.6 us
    dot_general x1, matrix products, local(): jnp.einsum('eth,elh->tl', grad_up, up_weight, preferred_element_type=jnp....  10.4 us
    dot_general x1, matrix products, local(): jnp.einsum('eth,elh->tl', weighted, down_weight, preferred_element_type=j...  7.62 us
    reduce_sum x1, other arithmetic, local(): score = jnp.sum(hidden * back * valid, axis=2).T  3.38 us

profile of v2, /device:TPU:0, one launch (start us, length us, event | category | flops | bytes accessed | tf_op | source)
XLA Modules:
  0.0 140.3 jit_solution(2392212315731996598)
XLA Ops:
  0.6 0.0 copy-start
  0.6 0.9 select_reduce_fusion.1
  1.6 0.1 copy.25
  1.7 0.1 copy.26
  1.8 1.9 %concatenate.14 = bf16[128,2176]{1,0:T(8,128)(2,1)} concatenate(bf16[128,1024]{1,0:T(8,128)(2,1)} %param.7, bf16[128,1024]{1,0:T(8,128)(2,1)} %param.8, bf16[128,64]{1,0:T(8,128)(2,1)S(1)} %copy.25, bf16[128,64]{1,0:T(8,128)(2,1)S(1)} %copy.26), dimensions={1} | concatenate | bytes 1114112 | tf_op jit(solution)/shard_map/concatenate | solution.py:197
  3.7 1.1 copy-done.2
  4.7 31.4 %shard_map.94 = bf16[4,2,4,32,2176]{4,3,2,1,0:T(8,128)(2,1)S(1)} custom-call(bf16[4,32,2176]{2,1,0:T(8,128)(2,1)S(1)} %bitcast.50), custom_call_target="tpu_custom_call" | custom-call | tf_op jit(solution)/shard_map/pallas_call | solution.py:143
  36.2 8.9 %fusion.8 = f32[1024,1536]{0,1} fusion(bf16[1024,1536]{0,1:T(8,128)(2,1)} %bitcast.66, bf16[1024,2176]{1,0:T(8,128)(2,1)S(1)} %bitcast.44), kind=kOutput, calls=%fused_computation.16 | convolution fusion | flops 3221225472 | bytes 11534336
  45.1 1.9 %constant_dynamic-slice_fusion.1 = (bf16[1024,8]{1,0:T(8,128)(2,1)S(1)}, bf16[1024,8]{1,0:T(8,128)(2,1)}) fusion(bf16[1024,2176]{1,0:T(8,128)(2,1)} %bitcast.45, s32[]{:T(128)S(6)} %select_n.18, s32[]{:T(128)S(6)} %select_n.19), kind=kLoop, calls=%fused_computation.29 | loop fusion | bytes 65544 | tf_op jit(solution)/shard_map/dynamic_slice | solution.py:207
  47.0 1.0 copy.32
  48.1 0.1 copy.31
  48.3 5.2 %fusion.10 = f32[1024,1536]{0,1:S(1)} fusion(bf16[1024,1536]{0,1:T(8,128)(2,1)S(1)} %bitcast.43, bf16[1024,2176]{1,0:T(8,128)(2,1)} %bitcast.46), kind=kOutput, calls=%fused_computation.18 | convolution fusion | flops 3221225472 | bytes 11534336
  53.5 6.9 %fusion.12 = f32[1024,1536]{0,1:S(1)} fusion(bf16[1024,1536]{0,1:T(8,128)(2,1)S(1)} %bitcast.65, bf16[1024,2176]{1,0:T(8,128)(2,1)} %bitcast.47), kind=kOutput, calls=%fused_computation.20 | convolution fusion | flops 3221225472 | bytes 11534336
  60.4 3.4 %multiply_reduce_fusion = bf16[8,1024]{1,0:T(8,128)(2,1)S(1)} fusion(f32[8,1024,192]{1,2,0:T(8,128)S(1)} %bitcast.52, f32[8,1024]{1,0:T(8,128)S(1)} %compare_convert_fusion, f32[8,1024,192]{1,2,0:T(8,128)S(1)} %bitcast.54, f32[8,1024,192]{1,2,0:T(8,128)S(1)} %bitcast.57), kind=kLoop, calls=%fused_computation | loop fusion | flops 12574720 | bytes 18923520 | tf_op jit(solution)/shard_map/reduce_sum | solution.py:220
  63.8 0.8 copy.29
  64.7 2.6 %dynamic_update_slice.3 = bf16[1024,128]{1,0:T(8,128)(2,1)S(1)} dynamic-update-slice(bf16[1024,128]{1,0:T(8,128)(2,1)S(1)} %broadcast_in_dim.32, bf16[1024,8]{1,0:T(8,128)(2,1)} %copy.29, s32[]{:T(128)} %constant.3.clone.1, s32[]{:T(128)S(6)} %select_n.20) | dynamic-update-slice | bytes 32772 | tf_op jit(solution)/shard_map/dynamic_update_slice | solution.py:230
  67.4 10.4 %fusion.3 = f32[1024,1024,1]{1,0,2:T(8,128)} fusion(bf16[8,1024,192]{1,2,0:T(8,128)(2,1)S(1)} %copy-done, f32[8,1024,192]{1,2,0:T(8,128)} %bitcast.51, f32[8,1024]{1,0:T(8,128)S(1)} %add_bitcast_fusion, f32[8,1024,192]{1,2,0:T(8,128)} %bitcast.58), kind=kOutput, calls=%fused_computation.11 | convolution fusion | flops 3232235520 | bytes 19955712 | tf_op jit(solution)/shard_map/eth,elh->tl/dot_general | solution.py:228
  77.8 10.6 %fusion.1 = bf16[1024,1024]{1,0:T(8,128)(2,1)S(1)} fusion(f32[1024,1024,1]{1,0,2:T(8,128)} %fusion.3, bf16[8,1024,192]{1,2,0:T(8,128)(2,1)} %param.11, f32[8,1024,192]{1,2,0:T(8,128)} %bitcast.59, f32[8,1024,192]{1,2,0:T(8,128)S(1)} %bitcast.55, f32[8,1024,192]{1,2,0:T(8,128)S(1)} %bitcast.53, f32[8,1024]{1,0:T(8,128)S(1)} %add_bitcast_fusion), kind=kOutput, calls=%fused_computation.8 | convolution fusion | flops 3240624128 | bytes 28344320 | tf_op jit(solution)/shard_map/eth,elh->tl/dot_general | solution.py:227
  88.5 7.6 %bitcast_convert_fusion = bf16[1024,1024]{1,0:T(8,128)(2,1)S(1)} fusion(bf16[8,1024,192]{1,2,0:T(8,128)(2,1)} %param.13, f32[8,1024]{1,0:T(8,128)S(1)} %add_bitcast_fusion, f32[8,1024,192]{1,2,0:T(8,128)S(1)} %bitcast.56, f32[8,1024,192]{1,2,0:T(8,128)} %bitcast.60), kind=kOutput, calls=%fused_computation.9 | convolution fusion | flops 3233284096 | bytes 17858560 | tf_op jit(solution)/shard_map/eth,elh->tl/dot_general | solution.py:226
  96.1 0.4 pad_maximum_fusion.parts
  96.5 42.2 %shard_map.95 = bf16[4,32,2176]{2,1,0:T(8,128)(2,1)S(1)} custom-call(bf16[4,2,4,32,2176]{4,3,2,1,0:T(8,128)(2,1)S(1)} %pad_maximum_fusion.parts), custom_call_target="tpu_custom_call" | custom-call | tf_op jit(solution)/shard_map/pallas_call | solution.py:164
  138.7 0.9 fusion.17
  139.6 0.1 copy.33
  139.7 0.6 select_reduce_fusion
  (24 shorter events, 0.1 us)
Async XLA Ops:
  0.6 47.6 %copy-start = (bf16[8,1024,192]{1,2,0:T(8,128)(2,1)S(1)}, bf16[8,1024,192]{1,2,0:T(8,128)(2,1)}, u32[]{:S(2)}) copy-start(bf16[8,1024,192]{1,2,0:T(8,128)(2,1)} %param.12) | copy-start | bytes 9437188
  3.7 1.1 copy-start.2
  36.2 8.9 %copy-start.1 = (bf16[4,2,4,32,2176]{4,3,2,1,0:T(8,128)(2,1)}, bf16[4,2,4,32,2176]{4,3,2,1,0:T(8,128)(2,1)S(1)}, u32[]{:S(2)}) copy-start(bf16[4,2,4,32,2176]{4,3,2,1,0:T(8,128)(2,1)S(1)} %shard_map.94) | copy-start | bytes 13369348
  48.2 5.3 %copy-start.9 = (bf16[8,1024,192]{1,2,0:T(8,128)(2,1)S(1)}, bf16[8,1024,192]{1,2,0:T(8,128)(2,1)}, u32[]{:S(2)}) copy-start(bf16[8,1024,192]{1,2,0:T(8,128)(2,1)} %param.11) | copy-start | bytes 9437188
  53.5 6.9 %copy-start.5 = (f32[1024,1536]{0,1}, f32[1024,1536]{0,1:S(1)}, u32[]{:S(2)}) copy-start(f32[1024,1536]{0,1:S(1)} %fusion.10) | copy-start | bytes 18874372
  53.5 6.9 %copy-start.3 = (f32[1024,1536]{0,1:S(1)}, f32[1024,1536]{0,1}, u32[]{:S(2)}) copy-start(f32[1024,1536]{0,1} %fusion.8) | copy-start | bytes 18874372
  60.4 3.4 %copy-start.7 = (f32[1024,1536]{0,1}, f32[1024,1536]{0,1:S(1)}, u32[]{:S(2)}) copy-start(f32[1024,1536]{0,1:S(1)} %fusion.12) | copy-start | bytes 18874372
  67.4 10.5 %copy-start.4 = (f32[1024,1536]{0,1:S(1)}, f32[1024,1536]{0,1}, u32[]{:S(2)}) copy-start(f32[1024,1536]{0,1} %fusion.8) | copy-start | bytes 18874372
  67.4 10.5 %copy-start.6 = (f32[1024,1536]{0,1:S(1)}, f32[1024,1536]{0,1}, u32[]{:S(2)}) copy-start(f32[1024,1536]{0,1} %copy-done.5) | copy-start | bytes 18874372
  96.1 43.6 %copy-start.8 = (s32[128,8]{0,1:T(8,128)S(1)}, s32[128,8]{0,1:T(8,128)}, u32[]{:S(2)}) copy-start(s32[128,8]{0,1:T(8,128)} %param.9) | copy-start | bytes 12292

commit v3 on v2

--- a/solution.py
+++ b/solution.py
@@ -135,6 +135,83 @@
         copy.wait_send()
 
 
+def expert_kernel(
+    features, experts, tile, me_ref, got, gate, up, down, out, mixed_sum, grad_sum, wide_sum
+):
+    step = pl.program_id(0)
+    steps = pl.num_programs(0)
+    column = me_ref[0] * steps + step
+    across = (((1,), (0,)), ((), ()))
+    along = (((1,), (1,)), ((), ()))
+
+    def dot(a, b, dims):
+        return lax.dot_general(a, b, dims, preferred_element_type=jnp.float32)
+
+    @pl.when(step == 0)
+    def _():
+        mixed_sum[...] = jnp.zeros_like(mixed_sum)
+        grad_sum[...] = jnp.zeros_like(grad_sum)
+        wide_sum[...] = jnp.zeros_like(wide_sum)
+
+    for start in range(0, got.shape[0], tile):
+        rows = slice(start, start + tile)
+        tokens = got[rows, :features]
+        upstream = got[rows, features : 2 * features]
+        table = got[rows, 2 * features :].astype(jnp.float32)
+        lane = lax.broadcasted_iota(jnp.int32, table.shape, 1)
+        here = (lane == column) | (lane == column + experts)
+        weight = jnp.sum(jnp.where(here, table, 0.0), axis=1, keepdims=True)
+        gate_act = dot(tokens, gate[0], across)
+        up_act = dot(tokens, up[0], across)
+        back = dot(upstream, down[0], across)
+        sig = jax.nn.sigmoid(gate_act)
+        silu = gate_act * sig
+        hidden = silu * up_act
+        score = jnp.sum(hidden * back, axis=1, keepdims=True)
+        score = jnp.where(weight > 0, score, 0.0)
+        wide_sum[rows, :] += jnp.where(lane == column, score, 0.0)
+        weighted = (hidden * weight).astype(jnp.bfloat16)
+        back = back * weight
+        slope = sig + silu * (1.0 - sig)
+        grad_gate = (back * up_act * slope).astype(jnp.bfloat16)
+        grad_up = (back * silu).astype(jnp.bfloat16)
+        mixed_sum[rows, :] += dot(weighted, down[0], along)
+        grad_sum[rows, :] += dot(grad_gate, gate[0], along) + dot(grad_up, up[0], along)
+
+    @pl.when(step == steps - 1)
+    def _():
+        out[:, :features] = mixed_sum[...].astype(out.dtype)
+        out[:, features : 2 * features] = grad_sum[...].astype(out.dtype)
+        out[:, 2 * features :] = wide_sum[...].astype(out.dtype)
+
+
+def expert_rows(got, gate_weight, up_weight, down_weight, me, experts):
+    count, features, hidden = gate_weight.shape
+    rows, width = got.shape
+    tile = 256 if rows % 256 == 0 else rows
+    resident = pl.BlockSpec((rows, width), lambda i: (0, 0))
+    streamed = pl.BlockSpec((1, features, hidden), lambda i: (i, 0, 0))
+    return pl.pallas_call(
+        functools.partial(expert_kernel, features, experts, tile),
+        grid=(count,),
+        out_shape=jax.ShapeDtypeStruct((rows, width), got.dtype),
+        in_specs=[
+            pl.BlockSpec(memory_space=pltpu.SMEM),
+            resident,
+            streamed,
+            streamed,
+            streamed,
+        ],
+        out_specs=resident,
+        scratch_shapes=[
+            pltpu.VMEM((rows, features), jnp.float32),
+            pltpu.VMEM((rows, features), jnp.float32),
+            pltpu.VMEM((rows, width - 2 * features), jnp.float32),
+        ],
+        compiler_params=pltpu.CompilerParams(vmem_limit_bytes=50 << 20),
+    )(me.reshape(1).astype(jnp.int32), got, gate_weight, up_weight, down_weight)
+
+
 def gather_rows(payload, dp_count, groups):
     rows, width = payload.shape
     z_count = groups // 2
@@ -184,24 +261,8 @@
     return out.reshape(dp_count * quarter, width)
 
 
-def local(latents, out_grad, routes, route_weights, gate_weight, up_weight, down_weight):
-    features = latents.shape[1]
-    local_experts = gate_weight.shape[0]
-    groups = lax.axis_size("expert")
-    experts = local_experts * groups
-    me = lax.axis_index("expert")
-    hot = routes[:, :, None] == jnp.arange(experts, dtype=jnp.int32)[None, None, :]
-    table = jnp.sum(jnp.where(hot, route_weights[:, :, None], 0.0), axis=1)
-    high = table.astype(jnp.bfloat16)
-    low = (table - high.astype(jnp.float32)).astype(jnp.bfloat16)
-    payload = jnp.concatenate([latents, out_grad, high, low], axis=1)
-    dp_count = lax.axis_size("dp")
-    rows = latents.shape[0]
-    fits = rows % (16 * dp_count) == 0 and groups * payload.size * 2 <= WHOLE_BYTES
-    if fits:
-        got = gather_rows(payload, dp_count, groups)
-    else:
-        got = lax.all_gather(payload, "expert", axis=0, tiled=True)
+def dense_parts(got, gate_weight, up_weight, down_weight, me, experts):
+    local_experts, features = gate_weight.shape[:2]
     tokens = got[:, :features]
     upstream = got[:, features : 2 * features]
     mine_high = lax.dynamic_slice_in_dim(got, 2 * features + me * local_experts, local_experts, 1)
@@ -229,9 +290,30 @@
     wide = jnp.zeros((got.shape[0], 2 * experts), jnp.float32)
     wide = lax.dynamic_update_slice_in_dim(wide, score, me * local_experts, 1)
     parts = jnp.concatenate([mixed, grad, wide], axis=1).astype(jnp.bfloat16)
+    return parts
+
+
+def local(latents, out_grad, routes, route_weights, gate_weight, up_weight, down_weight):
+    features = latents.shape[1]
+    local_experts = gate_weight.shape[0]
+    groups = lax.axis_size("expert")
+    experts = local_experts * groups
+    me = lax.axis_index("expert")
+    hot = routes[:, :, None] == jnp.arange(experts, dtype=jnp.int32)[None, None, :]
+    table = jnp.sum(jnp.where(hot, route_weights[:, :, None], 0.0), axis=1)
+    high = table.astype(jnp.bfloat16)
+    low = (table - high.astype(jnp.float32)).astype(jnp.bfloat16)
+    payload = jnp.concatenate([latents, out_grad, high, low], axis=1)
+    dp_count = lax.axis_size("dp")
+    rows = latents.shape[0]
+    fits = rows % (16 * dp_count) == 0 and groups * payload.size * 2 <= WHOLE_BYTES
     if fits:
+        got = gather_rows(payload, dp_count, groups)
+        parts = expert_rows(got, gate_weight, up_weight, down_weight, me, experts)
         total = reduce_rows(parts, dp_count, groups)
     else:
+        got = lax.all_gather(payload, "expert", axis=0, tiled=True)
+        parts = dense_parts(got, gate_weight, up_weight, down_weight, me, experts)
         parts = parts.reshape(groups, rows, parts.shape[1])
         moved = lax.all_to_all(parts, "expert", split_axis=0, concat_axis=0, tiled=True)
         total = lax.psum(jnp.sum(moved.astype(jnp.float32), axis=0), "dp")

time: 141 us -> 136 us (0.965)
  matrix products: 49.7 us -> 0 us
  Pallas kernels: 73.6 us -> 110 us
  local copies, waits for them, and re-layouts: 10.8 us -> 23.3 us
  other arithmetic: 5.34 us -> 1.38 us
    pallas_call x0 -> x1, Pallas kernels: none -> 37.1 us  [expert_rows(): pl.pallas_call(functools.partial(expert_kernel, features, experts, tile),...]
    dot_general x3 -> x0, matrix products: 28.7 us -> none  [the longest x1 10.6 us: local(): jnp.einsum('eth,elh->tl', grad_gate, gate_weight, preferred_element_type=...]
    unnamed x3 -> x0, matrix products: 21 us -> none
    unnamed x23 -> x12, local copies, waits for them, and re-layouts: 2.35 us -> 21 us
    reduce_sum x1 -> x0, other arithmetic: 3.38 us -> none  [local(): score = jnp.sum(hidden * back * valid, axis=2).T]
    dynamic_update_slice x1 -> x0, local copies, waits for them, and re-layouts: 2.64 us -> none  [local(): wide = lax.dynamic_update_slice_in_dim(wide, score, me * local_experts, 1)]
    dynamic_slice x1 -> x0, local copies, waits for them, and re-layouts: 1.94 us -> none  [local(): lax.dynamic_slice_in_dim(got, 2 * features + me * local_experts, local_ex...]
where the time goes in v3:
time: 136 us; the launch traced here: 135 us
  Pallas kernels  110 us (81%)
  local copies, waits for them, and re-layouts  23.3 us (17%)
  other arithmetic  1.38 us (1%)
    pallas_call x1, Pallas kernels, reduce_rows(): pl.pallas_call(functools.partial(reduce_kernel, dp_count, z_count), out_s...  41.3 us
    pallas_call x1, Pallas kernels, expert_rows(): pl.pallas_call(functools.partial(expert_kernel, features, experts, tile),...  37.1 us
    pallas_call x1, Pallas kernels, gather_rows(): pl.pallas_call(functools.partial(gather_kernel, dp_count, z_count), out_s...  31.5 us
    unnamed x12, local copies, waits for them, and re-layouts  21 us

profile of v3, /device:TPU:0, one launch (start us, length us, event | category | flops | bytes accessed | tf_op | source)
XLA Modules:
  0.0 135.3 jit_solution(16395444272149747113)
XLA Ops:
  0.6 0.7 select_reduce_fusion.1
  1.4 0.1 copy.22
  1.5 0.1 copy.21
  1.6 1.2 concatenate.3
  2.9 31.5 %shard_map.94 = bf16[4,2,4,32,2176]{4,3,2,1,0:T(8,128)(2,1)S(1)} custom-call(bf16[4,32,2176]{2,1,0:T(8,128)(2,1)S(1)} %bitcast.9), custom_call_target="tpu_custom_call" | custom-call | tf_op jit(solution)/shard_map/pallas_call | solution.py:220
  34.4 0.0 copy-start
  34.4 2.0 %copy-done = bf16[4,2,4,32,2176]{4,3,2,1,0:T(8,128)(2,1)} copy-done((bf16[4,2,4,32,2176]{4,3,2,1,0:T(8,128)(2,1)}, bf16[4,2,4,32,2176]{4,3,2,1,0:T(8,128)(2,1)S(1)}, u32[]{:S(2)}) %copy-start) | copy-done | bytes 4456472
  36.4 0.0 copy-start.2
  36.4 6.3 %copy.23.gate = bf16[8,1024,192]{2,1,0:T(8,128)(2,1)} copy(bf16[8,1024,192]{1,2,0:T(8,128)(2,1)} %param.11) | data formatting | bytes 6291456 | tf_op args[4]
  42.8 0.0 copy-done.2
  42.8 4.1 %copy.24.up = bf16[8,1024,192]{2,1,0:T(8,128)(2,1)} copy(bf16[8,1024,192]{1,2,0:T(8,128)(2,1)S(1)} %copy-done.2) | data formatting | bytes 6291456 | tf_op args[5]
  46.9 6.1 %copy.25.down = bf16[8,1024,192]{2,1,0:T(8,128)(2,1)} copy(bf16[8,1024,192]{1,2,0:T(8,128)(2,1)} %param.13) | data formatting | bytes 6291456 | tf_op args[6]
  53.0 37.1 %shard_map.95 = bf16[1024,2176]{1,0:T(8,128)(2,1)} custom-call(s32[1]{0:T(128)} %bitcast.me_ref, bf16[1024,2176]{1,0:T(8,128)(2,1)} %bitcast.5, bf16[8,1024,192]{2,1,0:T(8,128)(2,1)} %copy.23.gate, bf16[8,1024,192]{2,1,0:T(8,128)(2,1)} %copy.24.up, bf16[8,1024,192]{2,1,0:T(8,128)(2,1)} %copy.25.down), custom_call_target="tpu_custom_call" | custom-call | tf_op jit(solution)/shard_map/pallas_call | solution.py:194
  90.1 0.0 copy-start.1
  90.1 2.3 %copy-done.1 = bf16[1024,2176]{1,0:T(8,128)(2,1)S(1)} copy-done((bf16[1024,2176]{1,0:T(8,128)(2,1)S(1)}, bf16[1024,2176]{1,0:T(8,128)(2,1)}, u32[]{:S(2)}) %copy-start.1) | copy-done | bytes 4456472
  92.4 0.0 copy-start.3
  92.4 41.3 %shard_map.96 = bf16[4,32,2176]{2,1,0:T(8,128)(2,1)S(1)} custom-call(bf16[4,2,4,32,2176]{4,3,2,1,0:T(8,128)(2,1)S(1)} %bitcast.6), custom_call_target="tpu_custom_call" | custom-call | tf_op jit(solution)/shard_map/pallas_call | solution.py:241
  133.7 0.9 fusion
  134.6 0.1 copy.27
  134.7 0.0 copy-done.3
  134.7 0.6 select_reduce_fusion
  (3 shorter events, 0.0 us)
Async XLA Ops:
  34.4 2.0 %copy-start = (bf16[4,2,4,32,2176]{4,3,2,1,0:T(8,128)(2,1)}, bf16[4,2,4,32,2176]{4,3,2,1,0:T(8,128)(2,1)S(1)}, u32[]{:S(2)}) copy-start(bf16[4,2,4,32,2176]{4,3,2,1,0:T(8,128)(2,1)S(1)} %shard_map.94) | copy-start | bytes 13369348
  36.4 6.3 %copy-start.2 = (bf16[8,1024,192]{1,2,0:T(8,128)(2,1)S(1)}, bf16[8,1024,192]{1,2,0:T(8,128)(2,1)}, u32[]{:S(2)}) copy-start(bf16[8,1024,192]{1,2,0:T(8,128)(2,1)} %param.12) | copy-start | bytes 9437188
  90.1 2.3 %copy-start.1 = (bf16[1024,2176]{1,0:T(8,128)(2,1)S(1)}, bf16[1024,2176]{1,0:T(8,128)(2,1)}, u32[]{:S(2)}) copy-start(bf16[1024,2176]{1,0:T(8,128)(2,1)} %shard_map.95) | copy-start | bytes 13369348
  92.4 42.3 %copy-start.3 = (s32[128,8]{0,1:T(8,128)S(1)}, s32[128,8]{0,1:T(8,128)}, u32[]{:S(2)}) copy-start(s32[128,8]{0,1:T(8,128)} %param.9) | copy-start | bytes 12292

commit v4 on v3

--- a/solution.py
+++ b/solution.py
@@ -141,8 +141,8 @@
     step = pl.program_id(0)
     steps = pl.num_programs(0)
     column = me_ref[0] * steps + step
-    across = (((1,), (0,)), ((), ()))
-    along = (((1,), (1,)), ((), ()))
+    across = (((1,), (1,)), ((), ()))
+    along = (((1,), (0,)), ((), ()))
 
     def dot(a, b, dims):
         return lax.dot_general(a, b, dims, preferred_element_type=jnp.float32)
@@ -190,7 +190,8 @@
     rows, width = got.shape
     tile = 256 if rows % 256 == 0 else rows
     resident = pl.BlockSpec((rows, width), lambda i: (0, 0))
-    streamed = pl.BlockSpec((1, features, hidden), lambda i: (i, 0, 0))
+    streamed = pl.BlockSpec((1, hidden, features), lambda i: (i, 0, 0))
+    turned = [jnp.swapaxes(w, 1, 2) for w in (gate_weight, up_weight, down_weight)]
     return pl.pallas_call(
         functools.partial(expert_kernel, features, experts, tile),
         grid=(count,),
@@ -209,7 +210,7 @@
             pltpu.VMEM((rows, width - 2 * features), jnp.float32),
         ],
         compiler_params=pltpu.CompilerParams(vmem_limit_bytes=50 << 20),
-    )(me.reshape(1).astype(jnp.int32), got, gate_weight, up_weight, down_weight)
+    )(me.reshape(1).astype(jnp.int32), got, *turned)
 
 
 def gather_rows(payload, dp_count, groups):

time: 136 us -> 120 us (0.88)
  local copies, waits for them, and re-layouts: 23.3 us -> 8.58 us
    unnamed x12 -> x11, local copies, waits for them, and re-layouts: 21 us -> 5.44 us
where the time goes in v4:
time: 120 us
  Pallas kernels  109 us (91%)
  local copies, waits for them, and re-layouts  8.58 us (7%)
  other arithmetic  1.38 us (1%)
    pallas_call x1, Pallas kernels, reduce_rows(): pl.pallas_call(functools.partial(reduce_kernel, dp_count, z_count), out_s...  41.3 us
    pallas_call x1, Pallas kernels, expert_rows(): pl.pallas_call(functools.partial(expert_kernel, features, experts, tile),...  36.7 us
    pallas_call x1, Pallas kernels, gather_rows(): pl.pallas_call(functools.partial(gather_kernel, dp_count, z_count), out_s...  31.4 us
    unnamed x11, local copies, waits for them, and re-layouts  5.44 us

profile of v4, /device:TPU:0, one launch (start us, length us, event | category | flops | bytes accessed | tf_op | source)
XLA Modules:
  0.0 120.1 jit_solution(3457597536146645043)
XLA Ops:
  0.6 0.7 select_reduce_fusion.1
  1.4 0.0 copy-start.2
  1.4 0.1 copy.16
  1.5 0.1 copy.15
  1.6 2.0 %concatenate.3 = bf16[128,2176]{1,0:T(8,128)(2,1)} concatenate(bf16[128,1024]{1,0:T(8,128)(2,1)} %param.7, bf16[128,1024]{1,0:T(8,128)(2,1)} %param.8, bf16[128,64]{1,0:T(8,128)(2,1)S(1)} %copy.15, bf16[128,64]{1,0:T(8,128)(2,1)S(1)} %copy.16), dimensions={1} | concatenate | bytes 1114112 | tf_op jit(solution)/shard_map/concatenate | solution.py:307
  3.7 0.0 copy-start.3
  3.7 1.1 copy-done.3
  4.7 31.4 %shard_map.94 = bf16[4,2,4,32,2176]{4,3,2,1,0:T(8,128)(2,1)S(1)} custom-call(bf16[4,32,2176]{2,1,0:T(8,128)(2,1)S(1)} %bitcast.13), custom_call_target="tpu_custom_call" | custom-call | tf_op jit(solution)/shard_map/pallas_call | solution.py:221
  36.2 0.0 copy-start
  36.2 2.0 %copy-done = bf16[4,2,4,32,2176]{4,3,2,1,0:T(8,128)(2,1)} copy-done((bf16[4,2,4,32,2176]{4,3,2,1,0:T(8,128)(2,1)}, bf16[4,2,4,32,2176]{4,3,2,1,0:T(8,128)(2,1)S(1)}, u32[]{:S(2)}) %copy-start) | copy-done | bytes 4456472
  38.2 0.0 copy-done.2
  38.2 36.7 %shard_map.95 = bf16[1024,2176]{1,0:T(8,128)(2,1)} custom-call(s32[1]{0:T(128)} %bitcast.me_ref, bf16[1024,2176]{1,0:T(8,128)(2,1)} %bitcast.8, bf16[8,192,1024]{2,1,0:T(8,128)(2,1)S(1)} %bitcast.10, bf16[8,192,1024]{2,1,0:T(8,128)(2,1)} %bitcast.14, bf16[8,192,1024]{2,1,0:T(8,128)(2,1)} %bitcast.15), custom_call_target="tpu_custom_call" | custom-call | tf_op jit(solution)/shard_map/pallas_call | solution.py:195
  74.9 0.0 copy-start.1
  74.9 2.3 %copy-done.1 = bf16[1024,2176]{1,0:T(8,128)(2,1)S(1)} copy-done((bf16[1024,2176]{1,0:T(8,128)(2,1)S(1)}, bf16[1024,2176]{1,0:T(8,128)(2,1)}, u32[]{:S(2)}) %copy-start.1) | copy-done | bytes 4456472
  77.1 0.0 copy-start.4
  77.1 41.3 %shard_map.96 = bf16[4,32,2176]{2,1,0:T(8,128)(2,1)S(1)} custom-call(bf16[4,2,4,32,2176]{4,3,2,1,0:T(8,128)(2,1)S(1)} %bitcast.9), custom_call_target="tpu_custom_call" | custom-call | tf_op jit(solution)/shard_map/pallas_call | solution.py:242
  118.5 0.9 fusion
  119.3 0.1 copy.18
  119.4 0.0 copy-done.4
  119.5 0.6 select_reduce_fusion
  (3 shorter events, 0.0 us)
Async XLA Ops:
  1.4 36.8 %copy-start.2 = (bf16[8,1024,192]{1,2,0:T(8,128)(2,1)S(1)}, bf16[8,1024,192]{1,2,0:T(8,128)(2,1)}, u32[]{:S(2)}) copy-start(bf16[8,1024,192]{1,2,0:T(8,128)(2,1)} %param.11) | copy-start | bytes 9437188
  3.7 1.1 copy-start.3
  36.2 2.0 %copy-start = (bf16[4,2,4,32,2176]{4,3,2,1,0:T(8,128)(2,1)}, bf16[4,2,4,32,2176]{4,3,2,1,0:T(8,128)(2,1)S(1)}, u32[]{:S(2)}) copy-start(bf16[4,2,4,32,2176]{4,3,2,1,0:T(8,128)(2,1)S(1)} %shard_map.94) | copy-start | bytes 13369348
  74.9 2.3 %copy-start.1 = (bf16[1024,2176]{1,0:T(8,128)(2,1)S(1)}, bf16[1024,2176]{1,0:T(8,128)(2,1)}, u32[]{:S(2)}) copy-start(bf16[1024,2176]{1,0:T(8,128)(2,1)} %shard_map.95) | copy-start | bytes 13369348
  77.1 42.3 %copy-start.4 = (s32[128,8]{0,1:T(8,128)S(1)}, s32[128,8]{0,1:T(8,128)}, u32[]{:S(2)}) copy-start(s32[128,8]{0,1:T(8,128)} %param.9) | copy-start | bytes 12292

commit v5 on v4

--- a/solution.py
+++ b/solution.py
@@ -188,7 +188,7 @@
 def expert_rows(got, gate_weight, up_weight, down_weight, me, experts):
     count, features, hidden = gate_weight.shape
     rows, width = got.shape
-    tile = 256 if rows % 256 == 0 else rows
+    tile = 512 if rows % 512 == 0 else rows
     resident = pl.BlockSpec((rows, width), lambda i: (0, 0))
     streamed = pl.BlockSpec((1, hidden, features), lambda i: (i, 0, 0))
     turned = [jnp.swapaxes(w, 1, 2) for w in (gate_weight, up_weight, down_weight)]

time: 120 us -> 118 us (0.983)
  Pallas kernels: 109 us -> 107 us
    pallas_call x1, Pallas kernels: 36.7 us -> 34.7 us  [expert_rows(): pl.pallas_call(functools.partial(expert_kernel, features, experts, tile),...]
where the time goes in v5:
time: 118 us
  Pallas kernels  107 us (91%)
  local copies, waits for them, and re-layouts  8.58 us (7%)
  other arithmetic  1.38 us (1%)
    pallas_call x1, Pallas kernels, reduce_rows(): pl.pallas_call(functools.partial(reduce_kernel, dp_count, z_count), out_s...  41.3 us
    pallas_call x1, Pallas kernels, expert_rows(): pl.pallas_call(functools.partial(expert_kernel, features, experts, tile),...  34.7 us
    pallas_call x1, Pallas kernels, gather_rows(): pl.pallas_call(functools.partial(gather_kernel, dp_count, z_count), out_s...  31.4 us
    unnamed x11, local copies, waits for them, and re-layouts  5.44 us

profile of v5, /device:TPU:0, one launch (start us, length us, event | category | flops | bytes accessed | tf_op | source)
XLA Modules:
  0.0 118.2 jit_solution(12832332623108353351)
XLA Ops:
  0.6 0.7 select_reduce_fusion.1
  1.4 0.0 copy-start.2
  1.4 0.1 copy.16
  1.5 0.1 copy.15
  1.6 2.0 %concatenate.3 = bf16[128,2176]{1,0:T(8,128)(2,1)} concatenate(bf16[128,1024]{1,0:T(8,128)(2,1)} %param.7, bf16[128,1024]{1,0:T(8,128)(2,1)} %param.8, bf16[128,64]{1,0:T(8,128)(2,1)S(1)} %copy.15, bf16[128,64]{1,0:T(8,128)(2,1)S(1)} %copy.16), dimensions={1} | concatenate | bytes 1114112 | tf_op jit(solution)/shard_map/concatenate | solution.py:307
  3.7 0.0 copy-start.3
  3.7 1.1 copy-done.3
  4.7 31.4 %shard_map.94 = bf16[4,2,4,32,2176]{4,3,2,1,0:T(8,128)(2,1)S(1)} custom-call(bf16[4,32,2176]{2,1,0:T(8,128)(2,1)S(1)} %bitcast.13), custom_call_target="tpu_custom_call" | custom-call | tf_op jit(solution)/shard_map/pallas_call | solution.py:221
  36.2 0.0 copy-start
  36.2 2.0 %copy-done = bf16[4,2,4,32,2176]{4,3,2,1,0:T(8,128)(2,1)} copy-done((bf16[4,2,4,32,2176]{4,3,2,1,0:T(8,128)(2,1)}, bf16[4,2,4,32,2176]{4,3,2,1,0:T(8,128)(2,1)S(1)}, u32[]{:S(2)}) %copy-start) | copy-done | bytes 4456472
  38.2 0.0 copy-done.2
  38.2 34.7 %shard_map.95 = bf16[1024,2176]{1,0:T(8,128)(2,1)} custom-call(s32[1]{0:T(128)} %bitcast.me_ref, bf16[1024,2176]{1,0:T(8,128)(2,1)} %bitcast.8, bf16[8,192,1024]{2,1,0:T(8,128)(2,1)S(1)} %bitcast.10, bf16[8,192,1024]{2,1,0:T(8,128)(2,1)} %bitcast.14, bf16[8,192,1024]{2,1,0:T(8,128)(2,1)} %bitcast.15), custom_call_target="tpu_custom_call" | custom-call | tf_op jit(solution)/shard_map/pallas_call | solution.py:195
  72.9 0.0 copy-start.1
  72.9 2.3 %copy-done.1 = bf16[1024,2176]{1,0:T(8,128)(2,1)S(1)} copy-done((bf16[1024,2176]{1,0:T(8,128)(2,1)S(1)}, bf16[1024,2176]{1,0:T(8,128)(2,1)}, u32[]{:S(2)}) %copy-start.1) | copy-done | bytes 4456472
  75.2 0.0 copy-start.4
  75.2 41.3 %shard_map.96 = bf16[4,32,2176]{2,1,0:T(8,128)(2,1)S(1)} custom-call(bf16[4,2,4,32,2176]{4,3,2,1,0:T(8,128)(2,1)S(1)} %bitcast.9), custom_call_target="tpu_custom_call" | custom-call | tf_op jit(solution)/shard_map/pallas_call | solution.py:242
  116.6 0.9 fusion
  117.4 0.1 copy.18
  117.5 0.0 copy-done.4
  117.5 0.6 select_reduce_fusion
  (3 shorter events, 0.0 us)
Async XLA Ops:
  1.4 36.8 %copy-start.2 = (bf16[8,1024,192]{1,2,0:T(8,128)(2,1)S(1)}, bf16[8,1024,192]{1,2,0:T(8,128)(2,1)}, u32[]{:S(2)}) copy-start(bf16[8,1024,192]{1,2,0:T(8,128)(2,1)} %param.11) | copy-start | bytes 9437188
  3.7 1.1 copy-start.3
  36.2 2.0 %copy-start = (bf16[4,2,4,32,2176]{4,3,2,1,0:T(8,128)(2,1)}, bf16[4,2,4,32,2176]{4,3,2,1,0:T(8,128)(2,1)S(1)}, u32[]{:S(2)}) copy-start(bf16[4,2,4,32,2176]{4,3,2,1,0:T(8,128)(2,1)S(1)} %shard_map.94) | copy-start | bytes 13369348
  72.9 2.3 %copy-start.1 = (bf16[1024,2176]{1,0:T(8,128)(2,1)S(1)}, bf16[1024,2176]{1,0:T(8,128)(2,1)}, u32[]{:S(2)}) copy-start(bf16[1024,2176]{1,0:T(8,128)(2,1)} %shard_map.95) | copy-start | bytes 13369348
  75.2 42.3 %copy-start.4 = (s32[128,8]{0,1:T(8,128)S(1)}, s32[128,8]{0,1:T(8,128)}, u32[]{:S(2)}) copy-start(s32[128,8]{0,1:T(8,128)} %param.9) | copy-start | bytes 12292
